TPU v7x, 32 devices: a whole 2x2x4 slice. The times are simulated.
32 devices in a mesh: row: 2 (over core), circ: 4 (over z), rad: 4 (over y, x).
Axes of the slice: x: 2, y: 2, z: 4, core: 2. Of those that a mesh axis runs over, the one named last changes fastest.
Arguments:
- flow: float32 [2, 5, 8, 32, 512], P('row', None, None, 'rad', 'circ'), may hold values from -2 to 8, as said below
- inflow: float32 [5, 32, 512], P(None, 'rad', 'circ'), may hold values from -2 to 8, as said below
- outflow: float32 [5, 32, 512], P(None, 'rad', 'circ'), may hold values from -2 to 8, as said below
- wheel: float32 [32], P('rad'), may hold values from 0.3 to 0.7
- offsets: int32 [2], replicated, may hold values from 0 to 511
Outputs:
- advanced: float32 [2, 5, 8, 32, 512], P('row', None, None, 'rad', 'circ')
Inputs may be any that keep to these rules, and one draw needn't show every extreme that they name: Physical states: density positive, pressure positive, flow mainly axial. `inflow`: physical states, like flow. `outflow`: physical states, like flow.
All inputs are finite; a program needn't handle non-finite values.
Results may differ from a plain program's by a relative error of at most 0.00002.
Values sent between devices are 32-bit elements; how exact they have to be, the bound alone decides.
A program may use at most 64 MiB of HBM per device.

v0:
```python
import jax
import jax.numpy as jnp
from jax import lax
from jax.sharding import PartitionSpec as P

GAMMA = 1.4
COURANT = 0.1


def partner_2(shard, axis, distance):
    return lax.ppermute(shard, axis, [(i, i ^ 1 << distance) for i in range(lax.axis_size(axis))])


def with_halo(shard, sides, width, wrap):
    for axis, dim in sides:
        peers, length = (lax.axis_size(axis), shard.shape[dim])
        up = [(i, (i + 1) % peers) for i in range(peers if wrap else peers - 1)]
        down = [(j, i) for i, j in up]
        last = lax.slice_in_dim(shard, length - width, length, axis=dim)
        first = lax.slice_in_dim(shard, 0, width, axis=dim)
        before = lax.ppermute(last, axis, up)
        after = lax.ppermute(first, axis, down)
        shard = jnp.concatenate([before, shard, after], axis=dim)
    return shard


def unit_vector(index):
    values = [0.0, 0.0, 0.0, 0.0, 0.0]
    values[index] = 1.0
    return jnp.array(values, dtype=jnp.float32).reshape(5, 1, 1, 1)


def physical_flux(field, normal_axis):
    density = field[0]
    inverse = 1.0 / density
    velocity = field[1:4] * inverse
    kinetic = 0.5 * (field[1] * velocity[0] + field[2] * velocity[1] + field[3] * velocity[2])
    pressure = (GAMMA - 1.0) * (field[4] - kinetic)
    normal_vel = velocity[normal_axis]
    flux_terms = (
        field * normal_vel
        + pressure * unit_vector(1 + normal_axis)
        + pressure * normal_vel * unit_vector(4)
    )
    wave_speed = jnp.abs(normal_vel) + jnp.sqrt(GAMMA * pressure / density)
    return (flux_terms, wave_speed)


def face_flux(left_cells, right_cells, normal_axis):
    flux_left, speed_left = physical_flux(left_cells, normal_axis)
    flux_right, speed_right = physical_flux(right_cells, normal_axis)
    return 0.5 * (flux_left + flux_right) - 0.5 * jnp.maximum(speed_left, speed_right) * (
        right_cells - left_cells
    )


def divergence(axial_pad, radial_pad, circ_pad):
    flux_axial = face_flux(axial_pad[:, :-1], axial_pad[:, 1:], 0)
    flux_radial = face_flux(radial_pad[:, :, :-1], radial_pad[:, :, 1:], 1)
    flux_circ = face_flux(circ_pad[..., :-1], circ_pad[..., 1:], 2)
    total = (
        flux_axial[:, 1:]
        - flux_axial[:, :-1]
        + (flux_radial[:, :, 1:] - flux_radial[:, :, :-1])
        + (flux_circ[..., 1:] - flux_circ[..., :-1])
    )
    return -COURANT * total


def mirrored(layer):
    signs = jnp.array([1.0, 1.0, -1.0, 1.0, 1.0], dtype=jnp.float32).reshape(5, 1, 1, 1)
    return layer * signs


def reframe(layer, wheel, direction_sign):
    density = layer[0]
    swirl = layer[3]
    blade = wheel[:, None]
    new_swirl = swirl + direction_sign * density * blade
    new_energy = layer[4] + direction_sign * swirl * blade + 0.5 * density * blade * blade
    return jnp.stack([layer[0], layer[1], layer[2], new_swirl, new_energy])


def rotate_layer(partner, shift_cells):
    circ_cells = partner.shape[-1]
    cycle_size = lax.axis_size("circ")
    cycle_cells = circ_cells * cycle_size
    gathered = lax.all_gather(partner, "circ", axis=2, tiled=True)
    doubled = jnp.concatenate([gathered, gathered], axis=2)
    start = (lax.axis_index("circ") * circ_cells + shift_cells) % cycle_cells
    return lax.dynamic_slice_in_dim(doubled, start, circ_cells, 2)


def per_device(flow, inflow, outflow, wheel, offsets):
    field = flow[0]
    circ_cells = field.shape[-1]
    cycle_cells = circ_cells * lax.axis_size("circ")
    is_rotor = lax.axis_index("row") == 0
    rad_place = lax.axis_index("rad")
    rad_count = lax.axis_size("rad")
    sign_value = jnp.where(is_rotor, jnp.float32(-1.0), jnp.float32(1.0))

    def change_of(state, offset_now):
        own_layer = jnp.where(is_rotor, state[:, -1], state[:, 0])
        partner = partner_2(own_layer, "row", 0)
        shift_cells = jnp.where(is_rotor, offset_now, (cycle_cells - offset_now) % cycle_cells)
        ghost_layer = reframe(rotate_layer(partner, shift_cells), wheel, sign_value)
        lower_face = jnp.where(is_rotor, inflow, ghost_layer)
        upper_face = jnp.where(is_rotor, ghost_layer, outflow)
        circ_pad = with_halo(state, (("circ", 3),), 1, True)
        radial_rim = with_halo(state, (("rad", 2),), 1, False)
        low_side = jnp.where(rad_place == 0, mirrored(state[:, :, :1]), radial_rim[:, :, :1])
        high_side = jnp.where(
            rad_place == rad_count - 1, mirrored(state[:, :, -1:]), radial_rim[:, :, -1:]
        )
        radial_pad = jnp.concatenate([low_side, state, high_side], axis=2)
        axial_pad = jnp.concatenate([lower_face[:, None], state, upper_face[:, None]], axis=1)
        return divergence(axial_pad, radial_pad, circ_pad)

    def one_step(step, current):
        offset_now = offsets[step]
        first_section = current + change_of(current, offset_now)
        second_section = 0.75 * current + 0.25 * (
            first_section + change_of(first_section, offset_now)
        )
        return current / 3.0 + 2.0 / 3.0 * (second_section + change_of(second_section, offset_now))

    field = lax.fori_loop(0, offsets.shape[0], one_step, field)
    return field[None]


def solution(mesh):
    placed = (
        P("row", None, None, "rad", "circ"),
        P(None, "rad", "circ"),
        P(None, "rad", "circ"),
        P("rad"),
        P(),
    )
    return jax.shard_map(
        per_device,
        mesh=mesh,
        in_specs=placed,
        out_specs=P("row", None, None, "rad", "circ"),
        check_vma=False,
    )
```

profile of v0, /device:TPU:0, one launch (start us, length us, event | category | flops | bytes accessed | tf_op | source)
XLA Modules:
  0.0 164.1 jit_solution(3563433103882980642)
XLA Ops:
  0.1 0.8 copy-done.1
  1.0 162.5 %while.18 = (s32[]{:T(128)}, f32[5,8,8,128]{3,2,1,0:T(8,128)S(1)}, pred[]{:T(512)}, f32[5,8,128]{2,1,0:T(8,128)S(1)}, s32[2]{0:T(128)S(1)}, /*index=5*/f32[]{:T(...) while((s32[]{:T(128)}, f32[5,8,8,128]{3,2,1,0:T(8,128)S(1)}, ...), condition=%wide.region_1.2_spmd.clone.clone, body=%wide.region_0.1_spmd.sunk.clone.clone.sunk | while | flops 12460650 | bytes 31748420 | solution.py:128
  1.1 5.1 %collective-permute-start = (f32[5,8,8,1]{3,2,1,0:T(8,128)S(1)}, f32[5,8,8,1]{3,2,1,0:T(8,128)S(1)}, u32[]{:S(2)}, u32[]{:S(2)}) collective-permute-start(f32[5,8,8,1]{3,2,1,0:T(8,128)S(1)} %get-tuple-element.1782), channel_id=1, source_target_pairs={{4,0},{8,4},{12,8},{0,12},{5,1},{9,5},{13,9},{1,13},{6,2},{10,6},{... | collective-permute-start | bytes 3848 | tf_op jit(solution)/shard_map/while/body/eval_jaxpr/ppermute | solution.py:22
  6.2 1.3 collective-permute-start.2
  7.5 4.5 %collective-permute-start.3 = (f32[5,8,1,128]{3,2,1,0:T(1,128)S(1)}, f32[5,8,1,128]{3,2,1,0:T(1,128)S(1)}, u32[]{:S(2)}, u32[]{:S(2)}) collective-permute-start(f32[5,8,1,128]{3,2,1,0:T(1,128)S(1)} %get-tuple-element.1794), channel_id=1, source_target_pairs={{0,1},{1,2},{2,3},{4,5},{5,6},{6,7},{8,9},{9,10},{10,11},{12,13},{... | collective-permute-start | bytes 61448 | tf_op jit(solution)/shard_map/while/body/eval_jaxpr/ppermute | solution.py:21
  12.2 0.6 dynamic_slice.93
  14.5 0.1 multiply_bitcast_fusion.70
  14.8 0.2 multiply_subtract_fusion.12
  15.4 13.3 %all_gather.45 = f32[5,8,512]{2,1,0:T(8,128)S(1)} all-gather(f32[5,8,128]{2,1,0:T(8,128)S(1)} %collective-permute-done.4), channel_id=1, replica_groups=mesh['row'=2,'circ'=4,'rad'=4] {'circ'}, dimensions={2}, use_global_device_ids=true | all-gather | bytes 102400 | tf_op jit(solution)/shard_map/while/body/eval_jaxpr/all_gather | solution.py:88
  29.1 0.2 fusion.373
  29.4 0.1 multiply_subtract_fusion.13
  29.8 3.8 %collective-permute-start.5 = (f32[5,8,8,1]{3,2,1,0:T(8,128)S(1)}, f32[5,8,8,1]{3,2,1,0:T(8,128)S(1)}, u32[]{:S(2)}, u32[]{:S(2)}) collective-permute-start(f32[5,8,8,1]{3,2,1,0:T(8,128)S(1)} %get-tuple-element.1821), channel_id=1, source_target_pairs={{4,0},{8,4},{12,8},{0,12},{5,1},{9,5},{13,9},{1,13},{6,2},{10,6},{... | collective-permute-start | bytes 3848 | tf_op jit(solution)/shard_map/while/body/eval_jaxpr/ppermute | solution.py:22
  33.6 1.3 collective-permute-start.7
  34.9 4.9 %collective-permute-start.8 = (f32[5,8,1,128]{3,2,1,0:T(1,128)S(1)}, f32[5,8,1,128]{3,2,1,0:T(1,128)S(1)}, u32[]{:S(2)}, u32[]{:S(2)}) collective-permute-start(f32[5,8,1,128]{3,2,1,0:T(1,128)S(1)} %get-tuple-element.1837), channel_id=1, source_target_pairs={{0,1},{1,2},{2,3},{4,5},{5,6},{6,7},{8,9},{9,10},{10,11},{12,13},{... | collective-permute-start | bytes 61448 | tf_op jit(solution)/shard_map/while/body/eval_jaxpr/ppermute | solution.py:21
  39.9 0.8 collective-permute-done.6
  40.9 0.1 multiply_bitcast_fusion.79
  41.2 0.2 multiply_subtract_fusion.14
  41.4 13.2 %all_gather.46 = f32[5,8,512]{2,1,0:T(8,128)S(1)} all-gather(f32[5,8,128]{2,1,0:T(8,128)S(1)} %collective-permute-done.9), channel_id=1, replica_groups=mesh['row'=2,'circ'=4,'rad'=4] {'circ'}, dimensions={2}, use_global_device_ids=true | all-gather | bytes 102400 | tf_op jit(solution)/shard_map/while/body/eval_jaxpr/all_gather | solution.py:88
  55.4 0.2 fusion.385
  55.6 0.2 multiply_subtract_fusion.15
  55.8 0.1 fusion.390
  56.1 3.6 %collective-permute-start.10 = (f32[5,8,8,1]{3,2,1,0:T(8,128)S(1)}, f32[5,8,8,1]{3,2,1,0:T(8,128)S(1)}, u32[]{:S(2)}, u32[]{:S(2)}) collective-permute-start(f32[5,8,8,1]{3,2,1,0:T(8,128)S(1)} %get-tuple-element.1864), channel_id=1, source_target_pairs={{4,0},{8,4},{12,8},{0,12},{5,1},{9,5},{13,9},{1,13},{6,2},{10,6},{... | collective-permute-start | bytes 3848 | tf_op jit(solution)/shard_map/while/body/eval_jaxpr/ppermute | solution.py:22
  59.6 1.3 collective-permute-start.12
  60.9 5.4 %collective-permute-start.13 = (f32[5,8,1,128]{3,2,1,0:T(1,128)S(1)}, f32[5,8,1,128]{3,2,1,0:T(1,128)S(1)}, u32[]{:S(2)}, u32[]{:S(2)}) collective-permute-start(f32[5,8,1,128]{3,2,1,0:T(1,128)S(1)} %get-tuple-element.1880), channel_id=1, source_target_pairs={{0,1},{1,2},{2,3},{4,5},{5,6},{6,7},{8,9},{9,10},{10,11},{12,13},{... | collective-permute-start | bytes 61448 | tf_op jit(solution)/shard_map/while/body/eval_jaxpr/ppermute | solution.py:21
  66.5 0.3 collective-permute-done.11
  67.0 0.1 multiply_bitcast_fusion.87
  67.2 0.2 multiply_subtract_fusion.16
  67.5 0.1 collective-permute-done.14
  67.6 13.2 %all_gather.47 = f32[5,8,512]{2,1,0:T(8,128)S(1)} all-gather(f32[5,8,128]{2,1,0:T(8,128)S(1)} %collective-permute-done.14), channel_id=1, replica_groups=mesh['row'=2,'circ'=4,'rad'=4] {'circ'}, dimensions={2}, use_global_device_ids=true | all-gather | bytes 102400 | tf_op jit(solution)/shard_map/while/body/eval_jaxpr/all_gather | solution.py:88
  81.6 0.2 fusion.396
  81.8 0.2 multiply_subtract_fusion.17
  82.0 0.1 fusion.401
  82.2 3.9 %collective-permute-start = (f32[5,8,8,1]{3,2,1,0:T(8,128)S(1)}, f32[5,8,8,1]{3,2,1,0:T(8,128)S(1)}, u32[]{:S(2)}, u32[]{:S(2)}) collective-permute-start(f32[5,8,8,1]{3,2,1,0:T(8,128)S(1)} %get-tuple-element.1782), channel_id=1, source_target_pairs={{4,0},{8,4},{12,8},{0,12},{5,1},{9,5},{13,9},{1,13},{6,2},{10,6},{... | collective-permute-start | bytes 3848 | tf_op jit(solution)/shard_map/while/body/eval_jaxpr/ppermute | solution.py:22
  86.2 1.3 collective-permute-start.2
  87.5 5.4 %collective-permute-start.3 = (f32[5,8,1,128]{3,2,1,0:T(1,128)S(1)}, f32[5,8,1,128]{3,2,1,0:T(1,128)S(1)}, u32[]{:S(2)}, u32[]{:S(2)}) collective-permute-start(f32[5,8,1,128]{3,2,1,0:T(1,128)S(1)} %get-tuple-element.1794), channel_id=1, source_target_pairs={{0,1},{1,2},{2,3},{4,5},{5,6},{6,7},{8,9},{9,10},{10,11},{12,13},{... | collective-permute-start | bytes 61448 | tf_op jit(solution)/shard_map/while/body/eval_jaxpr/ppermute | solution.py:21
  93.0 0.6 dynamic_slice.93
  95.3 0.1 multiply_bitcast_fusion.70
  95.6 0.2 multiply_subtract_fusion.12
  96.2 13.3 %all_gather.45 = f32[5,8,512]{2,1,0:T(8,128)S(1)} all-gather(f32[5,8,128]{2,1,0:T(8,128)S(1)} %collective-permute-done.4), channel_id=1, replica_groups=mesh['row'=2,'circ'=4,'rad'=4] {'circ'}, dimensions={2}, use_global_device_ids=true | all-gather | bytes 102400 | tf_op jit(solution)/shard_map/while/body/eval_jaxpr/all_gather | solution.py:88
  110.0 0.2 fusion.373
  110.2 0.1 multiply_subtract_fusion.13
  110.6 3.8 %collective-permute-start.5 = (f32[5,8,8,1]{3,2,1,0:T(8,128)S(1)}, f32[5,8,8,1]{3,2,1,0:T(8,128)S(1)}, u32[]{:S(2)}, u32[]{:S(2)}) collective-permute-start(f32[5,8,8,1]{3,2,1,0:T(8,128)S(1)} %get-tuple-element.1821), channel_id=1, source_target_pairs={{4,0},{8,4},{12,8},{0,12},{5,1},{9,5},{13,9},{1,13},{6,2},{10,6},{... | collective-permute-start | bytes 3848 | tf_op jit(solution)/shard_map/while/body/eval_jaxpr/ppermute | solution.py:22
  114.4 1.3 collective-permute-start.7
  115.7 5.4 %collective-permute-start.8 = (f32[5,8,1,128]{3,2,1,0:T(1,128)S(1)}, f32[5,8,1,128]{3,2,1,0:T(1,128)S(1)}, u32[]{:S(2)}, u32[]{:S(2)}) collective-permute-start(f32[5,8,1,128]{3,2,1,0:T(1,128)S(1)} %get-tuple-element.1837), channel_id=1, source_target_pairs={{0,1},{1,2},{2,3},{4,5},{5,6},{6,7},{8,9},{9,10},{10,11},{12,13},{... | collective-permute-start | bytes 61448 | tf_op jit(solution)/shard_map/while/body/eval_jaxpr/ppermute | solution.py:21
  121.3 0.3 collective-permute-done.6
  121.7 0.1 multiply_bitcast_fusion.79
  122.0 0.2 multiply_subtract_fusion.14
  122.2 0.2 collective-permute-done.9
  122.4 13.2 %all_gather.46 = f32[5,8,512]{2,1,0:T(8,128)S(1)} all-gather(f32[5,8,128]{2,1,0:T(8,128)S(1)} %collective-permute-done.9), channel_id=1, replica_groups=mesh['row'=2,'circ'=4,'rad'=4] {'circ'}, dimensions={2}, use_global_device_ids=true | all-gather | bytes 102400 | tf_op jit(solution)/shard_map/while/body/eval_jaxpr/all_gather | solution.py:88
  136.4 0.2 fusion.385
  136.6 0.2 multiply_subtract_fusion.15
  136.8 0.1 fusion.390
  137.0 3.9 %collective-permute-start.10 = (f32[5,8,8,1]{3,2,1,0:T(8,128)S(1)}, f32[5,8,8,1]{3,2,1,0:T(8,128)S(1)}, u32[]{:S(2)}, u32[]{:S(2)}) collective-permute-start(f32[5,8,8,1]{3,2,1,0:T(8,128)S(1)} %get-tuple-element.1864), channel_id=1, source_target_pairs={{4,0},{8,4},{12,8},{0,12},{5,1},{9,5},{13,9},{1,13},{6,2},{10,6},{... | collective-permute-start | bytes 3848 | tf_op jit(solution)/shard_map/while/body/eval_jaxpr/ppermute | solution.py:22
  141.0 1.3 collective-permute-start.12
  142.3 5.4 %collective-permute-start.13 = (f32[5,8,1,128]{3,2,1,0:T(1,128)S(1)}, f32[5,8,1,128]{3,2,1,0:T(1,128)S(1)}, u32[]{:S(2)}, u32[]{:S(2)}) collective-permute-start(f32[5,8,1,128]{3,2,1,0:T(1,128)S(1)} %get-tuple-element.1880), channel_id=1, source_target_pairs={{0,1},{1,2},{2,3},{4,5},{5,6},{6,7},{8,9},{9,10},{10,11},{12,13},{... | collective-permute-start | bytes 61448 | tf_op jit(solution)/shard_map/while/body/eval_jaxpr/ppermute | solution.py:21
  147.8 0.3 collective-permute-done.11
  148.3 0.1 multiply_bitcast_fusion.87
  148.6 0.2 multiply_subtract_fusion.16
  148.8 0.2 collective-permute-done.14
  149.0 13.2 %all_gather.47 = f32[5,8,512]{2,1,0:T(8,128)S(1)} all-gather(f32[5,8,128]{2,1,0:T(8,128)S(1)} %collective-permute-done.14), channel_id=1, replica_groups=mesh['row'=2,'circ'=4,'rad'=4] {'circ'}, dimensions={2}, use_global_device_ids=true | all-gather | bytes 102400 | tf_op jit(solution)/shard_map/while/body/eval_jaxpr/all_gather | solution.py:88
  162.9 0.2 fusion.396
  163.2 0.2 multiply_subtract_fusion.17
  163.3 0.1 fusion.401
  163.5 0.7 copy-done
  (207 shorter events, 7.9 us)
Async XLA Ops:
  0.0 0.9 copy-start.1
  0.0 0.9 copy-start.3
  0.0 0.9 copy-start.9
  0.0 0.9 copy-start.10
  0.0 0.9 copy-start.2
  0.0 0.9 copy-start.7
  0.0 0.9 copy-start.8
  0.1 0.9 copy-start.4
  0.1 0.9 copy-start.5
  0.1 0.9 copy-start.6
  1.1 13.1 %collective-permute-start = (f32[5,8,8,1]{3,2,1,0:T(8,128)S(1)}, f32[5,8,8,1]{3,2,1,0:T(8,128)S(1)}, u32[]{:S(2)}, u32[]{:S(2)}) collective-permute-start(f32[5,8,8,1]{3,2,1,0:T(8,128)S(1)} %get-tuple-element.1782), channel_id=1, source_target_pairs={{4,0},{8,4},{12,8},{0,12},{5,1},{9,5},{13,9},{1,13},{6,2},{10,6},{... | collective-permute-start | bytes 3848 | tf_op jit(solution)/shard_map/while/body/eval_jaxpr/ppermute | solution.py:22
  6.2 8.1 %collective-permute-start.1 = (f32[5,8,8,1]{3,2,1,0:T(8,128)S(1)}, f32[5,8,8,1]{3,2,1,0:T(8,128)S(1)}, u32[]{:S(2)}, u32[]{:S(2)}) collective-permute-start(f32[5,8,8,1]{3,2,1,0:T(8,128)S(1)} %get-tuple-element.1783), channel_id=1, source_target_pairs={{0,4},{4,8},{8,12},{12,0},{1,5},{5,9},{9,13},{13,1},{2,6},{6,10},{... | collective-permute-start | bytes 3848 | tf_op jit(solution)/shard_map/while/body/eval_jaxpr/ppermute | solution.py:21
  6.2 8.8 %collective-permute-start.2 = (f32[5,8,1,128]{3,2,1,0:T(1,128)S(1)}, f32[5,8,1,128]{3,2,1,0:T(1,128)S(1)}, u32[]{:S(2)}, u32[]{:S(2)}) collective-permute-start(f32[5,8,1,128]{3,2,1,0:T(1,128)S(1)} %get-tuple-element.1793), channel_id=1, source_target_pairs={{1,0},{2,1},{3,2},{5,4},{6,5},{7,6},{9,8},{10,9},{11,10},{13,12},{... | collective-permute-start | bytes 61448 | tf_op jit(solution)/shard_map/while/body/eval_jaxpr/ppermute | solution.py:22
  7.5 7.5 %collective-permute-start.3 = (f32[5,8,1,128]{3,2,1,0:T(1,128)S(1)}, f32[5,8,1,128]{3,2,1,0:T(1,128)S(1)}, u32[]{:S(2)}, u32[]{:S(2)}) collective-permute-start(f32[5,8,1,128]{3,2,1,0:T(1,128)S(1)} %get-tuple-element.1794), channel_id=1, source_target_pairs={{0,1},{1,2},{2,3},{4,5},{5,6},{6,7},{8,9},{9,10},{10,11},{12,13},{... | collective-permute-start | bytes 61448 | tf_op jit(solution)/shard_map/while/body/eval_jaxpr/ppermute | solution.py:21
  12.1 3.2 %collective-permute-start.4 = (f32[5,8,128]{2,1,0:T(8,128)S(1)}, f32[5,8,128]{2,1,0:T(8,128)S(1)}, u32[]{:S(2)}, u32[]{:S(2)}) collective-permute-start(f32[5,8,128]{2,1,0:T(8,128)S(1)} %fusion.374), channel_id=1, source_target_pairs={{0,16},{16,0},{1,17},{17,1},{2,18},{18,2},{3,19},{19,3},{4,20},{20... | collective-permute-start | bytes 61448 | tf_op jit(solution)/shard_map/while/body/eval_jaxpr/ppermute | solution.py:11
  29.8 10.1 %collective-permute-start.5 = (f32[5,8,8,1]{3,2,1,0:T(8,128)S(1)}, f32[5,8,8,1]{3,2,1,0:T(8,128)S(1)}, u32[]{:S(2)}, u32[]{:S(2)}) collective-permute-start(f32[5,8,8,1]{3,2,1,0:T(8,128)S(1)} %get-tuple-element.1821), channel_id=1, source_target_pairs={{4,0},{8,4},{12,8},{0,12},{5,1},{9,5},{13,9},{1,13},{6,2},{10,6},{... | collective-permute-start | bytes 3848 | tf_op jit(solution)/shard_map/while/body/eval_jaxpr/ppermute | solution.py:22
  33.6 7.1 %collective-permute-start.6 = (f32[5,8,8,1]{3,2,1,0:T(8,128)S(1)}, f32[5,8,8,1]{3,2,1,0:T(8,128)S(1)}, u32[]{:S(2)}, u32[]{:S(2)}) collective-permute-start(f32[5,8,8,1]{3,2,1,0:T(8,128)S(1)} %get-tuple-element.1822), channel_id=1, source_target_pairs={{0,4},{4,8},{8,12},{12,0},{1,5},{5,9},{9,13},{13,1},{2,6},{6,10},{... | collective-permute-start | bytes 3848 | tf_op jit(solution)/shard_map/while/body/eval_jaxpr/ppermute | solution.py:21
  33.6 21.2 %collective-permute-start.7 = (f32[5,8,1,128]{3,2,1,0:T(1,128)S(1)}, f32[5,8,1,128]{3,2,1,0:T(1,128)S(1)}, u32[]{:S(2)}, u32[]{:S(2)}) collective-permute-start(f32[5,8,1,128]{3,2,1,0:T(1,128)S(1)} %get-tuple-element.1836), channel_id=1, source_target_pairs={{1,0},{2,1},{3,2},{5,4},{6,5},{7,6},{9,8},{10,9},{11,10},{13,12},{... | collective-permute-start | bytes 61448 | tf_op jit(solution)/shard_map/while/body/eval_jaxpr/ppermute | solution.py:22
  34.9 19.9 %collective-permute-start.8 = (f32[5,8,1,128]{3,2,1,0:T(1,128)S(1)}, f32[5,8,1,128]{3,2,1,0:T(1,128)S(1)}, u32[]{:S(2)}, u32[]{:S(2)}) collective-permute-start(f32[5,8,1,128]{3,2,1,0:T(1,128)S(1)} %get-tuple-element.1837), channel_id=1, source_target_pairs={{0,1},{1,2},{2,3},{4,5},{5,6},{6,7},{8,9},{9,10},{10,11},{12,13},{... | collective-permute-start | bytes 61448 | tf_op jit(solution)/shard_map/while/body/eval_jaxpr/ppermute | solution.py:21
  39.8 1.6 collective-permute-start.9
  56.1 10.4 %collective-permute-start.10 = (f32[5,8,8,1]{3,2,1,0:T(8,128)S(1)}, f32[5,8,8,1]{3,2,1,0:T(8,128)S(1)}, u32[]{:S(2)}, u32[]{:S(2)}) collective-permute-start(f32[5,8,8,1]{3,2,1,0:T(8,128)S(1)} %get-tuple-element.1864), channel_id=1, source_target_pairs={{4,0},{8,4},{12,8},{0,12},{5,1},{9,5},{13,9},{1,13},{6,2},{10,6},{... | collective-permute-start | bytes 3848 | tf_op jit(solution)/shard_map/while/body/eval_jaxpr/ppermute | solution.py:22
  59.6 7.1 %collective-permute-start.11 = (f32[5,8,8,1]{3,2,1,0:T(8,128)S(1)}, f32[5,8,8,1]{3,2,1,0:T(8,128)S(1)}, u32[]{:S(2)}, u32[]{:S(2)}) collective-permute-start(f32[5,8,8,1]{3,2,1,0:T(8,128)S(1)} %get-tuple-element.1865), channel_id=1, source_target_pairs={{0,4},{4,8},{8,12},{12,0},{1,5},{5,9},{9,13},{13,1},{2,6},{6,10},{... | collective-permute-start | bytes 3848 | tf_op jit(solution)/shard_map/while/body/eval_jaxpr/ppermute | solution.py:21
  59.6 21.3 %collective-permute-start.12 = (f32[5,8,1,128]{3,2,1,0:T(1,128)S(1)}, f32[5,8,1,128]{3,2,1,0:T(1,128)S(1)}, u32[]{:S(2)}, u32[]{:S(2)}) collective-permute-start(f32[5,8,1,128]{3,2,1,0:T(1,128)S(1)} %get-tuple-element.1879), channel_id=1, source_target_pairs={{1,0},{2,1},{3,2},{5,4},{6,5},{7,6},{9,8},{10,9},{11,10},{13,12},{... | collective-permute-start | bytes 61448 | tf_op jit(solution)/shard_map/while/body/eval_jaxpr/ppermute | solution.py:22
  60.9 20.0 %collective-permute-start.13 = (f32[5,8,1,128]{3,2,1,0:T(1,128)S(1)}, f32[5,8,1,128]{3,2,1,0:T(1,128)S(1)}, u32[]{:S(2)}, u32[]{:S(2)}) collective-permute-start(f32[5,8,1,128]{3,2,1,0:T(1,128)S(1)} %get-tuple-element.1880), channel_id=1, source_target_pairs={{0,1},{1,2},{2,3},{4,5},{5,6},{6,7},{8,9},{9,10},{10,11},{12,13},{... | collective-permute-start | bytes 61448 | tf_op jit(solution)/shard_map/while/body/eval_jaxpr/ppermute | solution.py:21
  66.4 1.3 collective-permute-start.14
  82.2 12.8 %collective-permute-start = (f32[5,8,8,1]{3,2,1,0:T(8,128)S(1)}, f32[5,8,8,1]{3,2,1,0:T(8,128)S(1)}, u32[]{:S(2)}, u32[]{:S(2)}) collective-permute-start(f32[5,8,8,1]{3,2,1,0:T(8,128)S(1)} %get-tuple-element.1782), channel_id=1, source_target_pairs={{4,0},{8,4},{12,8},{0,12},{5,1},{9,5},{13,9},{1,13},{6,2},{10,6},{... | collective-permute-start | bytes 3848 | tf_op jit(solution)/shard_map/while/body/eval_jaxpr/ppermute | solution.py:22
  86.1 9.0 %collective-permute-start.1 = (f32[5,8,8,1]{3,2,1,0:T(8,128)S(1)}, f32[5,8,8,1]{3,2,1,0:T(8,128)S(1)}, u32[]{:S(2)}, u32[]{:S(2)}) collective-permute-start(f32[5,8,8,1]{3,2,1,0:T(8,128)S(1)} %get-tuple-element.1783), channel_id=1, source_target_pairs={{0,4},{4,8},{8,12},{12,0},{1,5},{5,9},{9,13},{13,1},{2,6},{6,10},{... | collective-permute-start | bytes 3848 | tf_op jit(solution)/shard_map/while/body/eval_jaxpr/ppermute | solution.py:21
  86.2 9.7 %collective-permute-start.2 = (f32[5,8,1,128]{3,2,1,0:T(1,128)S(1)}, f32[5,8,1,128]{3,2,1,0:T(1,128)S(1)}, u32[]{:S(2)}, u32[]{:S(2)}) collective-permute-start(f32[5,8,1,128]{3,2,1,0:T(1,128)S(1)} %get-tuple-element.1793), channel_id=1, source_target_pairs={{1,0},{2,1},{3,2},{5,4},{6,5},{7,6},{9,8},{10,9},{11,10},{13,12},{... | collective-permute-start | bytes 61448 | tf_op jit(solution)/shard_map/while/body/eval_jaxpr/ppermute | solution.py:22
  87.5 8.4 %collective-permute-start.3 = (f32[5,8,1,128]{3,2,1,0:T(1,128)S(1)}, f32[5,8,1,128]{3,2,1,0:T(1,128)S(1)}, u32[]{:S(2)}, u32[]{:S(2)}) collective-permute-start(f32[5,8,1,128]{3,2,1,0:T(1,128)S(1)} %get-tuple-element.1794), channel_id=1, source_target_pairs={{0,1},{1,2},{2,3},{4,5},{5,6},{6,7},{8,9},{9,10},{10,11},{12,13},{... | collective-permute-start | bytes 61448 | tf_op jit(solution)/shard_map/while/body/eval_jaxpr/ppermute | solution.py:21
  92.9 3.2 %collective-permute-start.4 = (f32[5,8,128]{2,1,0:T(8,128)S(1)}, f32[5,8,128]{2,1,0:T(8,128)S(1)}, u32[]{:S(2)}, u32[]{:S(2)}) collective-permute-start(f32[5,8,128]{2,1,0:T(8,128)S(1)} %fusion.374), channel_id=1, source_target_pairs={{0,16},{16,0},{1,17},{17,1},{2,18},{18,2},{3,19},{19,3},{4,20},{20... | collective-permute-start | bytes 61448 | tf_op jit(solution)/shard_map/while/body/eval_jaxpr/ppermute | solution.py:11
  110.6 10.6 %collective-permute-start.5 = (f32[5,8,8,1]{3,2,1,0:T(8,128)S(1)}, f32[5,8,8,1]{3,2,1,0:T(8,128)S(1)}, u32[]{:S(2)}, u32[]{:S(2)}) collective-permute-start(f32[5,8,8,1]{3,2,1,0:T(8,128)S(1)} %get-tuple-element.1821), channel_id=1, source_target_pairs={{4,0},{8,4},{12,8},{0,12},{5,1},{9,5},{13,9},{1,13},{6,2},{10,6},{... | collective-permute-start | bytes 3848 | tf_op jit(solution)/shard_map/while/body/eval_jaxpr/ppermute | solution.py:22
  114.4 7.1 %collective-permute-start.6 = (f32[5,8,8,1]{3,2,1,0:T(8,128)S(1)}, f32[5,8,8,1]{3,2,1,0:T(8,128)S(1)}, u32[]{:S(2)}, u32[]{:S(2)}) collective-permute-start(f32[5,8,8,1]{3,2,1,0:T(8,128)S(1)} %get-tuple-element.1822), channel_id=1, source_target_pairs={{0,4},{4,8},{8,12},{12,0},{1,5},{5,9},{9,13},{13,1},{2,6},{6,10},{... | collective-permute-start | bytes 3848 | tf_op jit(solution)/shard_map/while/body/eval_jaxpr/ppermute | solution.py:21
  114.4 21.4 %collective-permute-start.7 = (f32[5,8,1,128]{3,2,1,0:T(1,128)S(1)}, f32[5,8,1,128]{3,2,1,0:T(1,128)S(1)}, u32[]{:S(2)}, u32[]{:S(2)}) collective-permute-start(f32[5,8,1,128]{3,2,1,0:T(1,128)S(1)} %get-tuple-element.1836), channel_id=1, source_target_pairs={{1,0},{2,1},{3,2},{5,4},{6,5},{7,6},{9,8},{10,9},{11,10},{13,12},{... | collective-permute-start | bytes 61448 | tf_op jit(solution)/shard_map/while/body/eval_jaxpr/ppermute | solution.py:22
  115.7 20.1 %collective-permute-start.8 = (f32[5,8,1,128]{3,2,1,0:T(1,128)S(1)}, f32[5,8,1,128]{3,2,1,0:T(1,128)S(1)}, u32[]{:S(2)}, u32[]{:S(2)}) collective-permute-start(f32[5,8,1,128]{3,2,1,0:T(1,128)S(1)} %get-tuple-element.1837), channel_id=1, source_target_pairs={{0,1},{1,2},{2,3},{4,5},{5,6},{6,7},{8,9},{9,10},{10,11},{12,13},{... | collective-permute-start | bytes 61448 | tf_op jit(solution)/shard_map/while/body/eval_jaxpr/ppermute | solution.py:21
  121.2 1.3 collective-permute-start.9
  137.0 10.8 %collective-permute-start.10 = (f32[5,8,8,1]{3,2,1,0:T(8,128)S(1)}, f32[5,8,8,1]{3,2,1,0:T(8,128)S(1)}, u32[]{:S(2)}, u32[]{:S(2)}) collective-permute-start(f32[5,8,8,1]{3,2,1,0:T(8,128)S(1)} %get-tuple-element.1864), channel_id=1, source_target_pairs={{4,0},{8,4},{12,8},{0,12},{5,1},{9,5},{13,9},{1,13},{6,2},{10,6},{... | collective-permute-start | bytes 3848 | tf_op jit(solution)/shard_map/while/body/eval_jaxpr/ppermute | solution.py:22
  140.9 7.1 %collective-permute-start.11 = (f32[5,8,8,1]{3,2,1,0:T(8,128)S(1)}, f32[5,8,8,1]{3,2,1,0:T(8,128)S(1)}, u32[]{:S(2)}, u32[]{:S(2)}) collective-permute-start(f32[5,8,8,1]{3,2,1,0:T(8,128)S(1)} %get-tuple-element.1865), channel_id=1, source_target_pairs={{0,4},{4,8},{8,12},{12,0},{1,5},{5,9},{9,13},{13,1},{2,6},{6,10},{... | collective-permute-start | bytes 3848 | tf_op jit(solution)/shard_map/while/body/eval_jaxpr/ppermute | solution.py:21
  141.0 21.4 %collective-permute-start.12 = (f32[5,8,1,128]{3,2,1,0:T(1,128)S(1)}, f32[5,8,1,128]{3,2,1,0:T(1,128)S(1)}, u32[]{:S(2)}, u32[]{:S(2)}) collective-permute-start(f32[5,8,1,128]{3,2,1,0:T(1,128)S(1)} %get-tuple-element.1879), channel_id=1, source_target_pairs={{1,0},{2,1},{3,2},{5,4},{6,5},{7,6},{9,8},{10,9},{11,10},{13,12},{... | collective-permute-start | bytes 61448 | tf_op jit(solution)/shard_map/while/body/eval_jaxpr/ppermute | solution.py:22
  142.3 20.1 %collective-permute-start.13 = (f32[5,8,1,128]{3,2,1,0:T(1,128)S(1)}, f32[5,8,1,128]{3,2,1,0:T(1,128)S(1)}, u32[]{:S(2)}, u32[]{:S(2)}) collective-permute-start(f32[5,8,1,128]{3,2,1,0:T(1,128)S(1)} %get-tuple-element.1880), channel_id=1, source_target_pairs={{0,1},{1,2},{2,3},{4,5},{5,6},{6,7},{8,9},{9,10},{10,11},{12,13},{... | collective-permute-start | bytes 61448 | tf_op jit(solution)/shard_map/while/body/eval_jaxpr/ppermute | solution.py:21
  147.7 1.3 collective-permute-start.14
  163.5 0.7 copy-start
where the time goes:
time: 165 us; the launch traced here: 164 us
  blocking collectives  79.3 us (48%)
  starting transfers between devices  63.5 us (38%)
  other arithmetic  11.7 us (7%)
  loops' own time  3.82 us (2%)
  local copies, waits for them, and re-layouts  3.59 us (2%)
  waiting for transfers between devices  2.13 us (1%)
    all_gather x6, blocking collectives, rotate_layer(): gathered = lax.all_gather(partner, 'circ', axis=2, tiled=True)  79.3 us
    ppermute x12, starting transfers between devices, with_halo(): after = lax.ppermute(first, axis, down)  31.8 us
    ppermute x12, starting transfers between devices, with_halo(): before = lax.ppermute(last, axis, up)  31.3 us
    another operation x1, loops' own time, per_device(): field = lax.fori_loop(0, offsets.shape[0], one_step, field)  3.82 us
    sub x18, other arithmetic, face_flux(): 0.5 * (flux_left + flux_right)  3.78 us
  transfers between devices with their start and end apart: 30, of which 7 were waited for; matrix products, arithmetic and copies ran while one was open for 4% of the time, Pallas kernels for 0%

commit v1 on v0

v1 whole, which is shorter than its diff:
```python
import functools

import jax
import jax.numpy as jnp
from jax import lax
from jax.experimental import pallas as pl
from jax.experimental.pallas import tpu as pltpu
from jax.sharding import PartitionSpec as P

GAMMA = 1.4
COURANT = 0.1
MESH = pl.DeviceIdType.MESH
STAGES = 3


def primitives(q):
    inverse = 1.0 / q[0]
    vel = [q[1] * inverse, q[2] * inverse, q[3] * inverse]
    kinetic = 0.5 * (q[1] * vel[0] + q[2] * vel[1] + q[3] * vel[2])
    pressure = (GAMMA - 1.0) * (q[4] - kinetic)
    sound = jnp.sqrt(GAMMA * pressure * inverse)
    return vel, pressure, sound


def normal_flux(q, prim, k):
    vel, pressure, sound = prim
    v = vel[k]
    f = [q[1 + k], q[1] * v, q[2] * v, q[3] * v, (q[4] + pressure) * v]
    f[1 + k] = f[1 + k] + pressure
    return f, jnp.abs(v) + sound


def jump(speed_a, speed_b, left, right):
    s = jnp.maximum(speed_a, speed_b)
    return [s * (right[c] - left[c]) for c in range(5)]


def kernel(
    nc, nr, steps,
    flow_ref, inflow_ref, outflow_ref, wheel_ref, offsets_ref,
    out_ref,
    state, far, gsend, grecv, csend, crecv, rsend, rrecv,
    gs_sem, gr_sem, hs_sem, hr_sem,
):
    ca, rows, cols = state.shape[2:]
    total = steps * STAGES
    row = lax.axis_index("row")
    me = lax.axis_index("circ")
    rad = lax.axis_index("rad")
    is_rotor = row == 0
    other = 1 - row
    right, left = lax.rem(me + 1, nc), lax.rem(me + nc - 1, nc)
    above, below = lax.rem(rad + 1, nr), lax.rem(rad + nr - 1, nr)

    barrier = pltpu.get_barrier_semaphore()
    for d in range(nc):
        pl.semaphore_signal(
            barrier, inc=1, device_id=(other, lax.rem(me + d, nc), rad), device_id_type=MESH)
    for peer in ((row, right, rad), (row, left, rad), (row, me, above), (row, me, below)):
        pl.semaphore_signal(barrier, inc=1, device_id=peer, device_id_type=MESH)

    lane = lax.broadcasted_iota(jnp.int32, (rows, cols), 1)
    sub = lax.broadcasted_iota(jnp.int32, (rows, cols), 0)
    first_lane, last_lane = lane == 0, lane == cols - 1
    first_sub, last_sub = sub == 0, sub == rows - 1
    wall_lo = jnp.logical_and(first_sub, rad == 0)
    wall_hi = jnp.logical_and(last_sub, rad == nr - 1)
    pair = lax.div(lane, 2)
    even = lax.rem(lane, 2) == 0
    sigma = jnp.where(is_rotor, jnp.float32(-1.0), jnp.float32(1.0))
    blade = jnp.zeros((rows, cols), jnp.float32)
    for r in range(rows):
        blade = jnp.where(sub == r, wheel_ref[r], blade)

    def axial(k):
        return jnp.where(is_rotor, ca - 1 - k, k)

    def gather_copy(slot, d):
        return pltpu.make_async_remote_copy(
            src_ref=gsend.at[slot], dst_ref=grecv.at[slot, me],
            send_sem=gs_sem.at[slot, d], recv_sem=gr_sem.at[slot, me],
            device_id=(other, lax.rem(me + d, nc), rad), device_id_type=MESH)

    def gather_arrival(slot, j):
        return pltpu.make_async_remote_copy(
            src_ref=gsend.at[slot], dst_ref=grecv.at[slot, j],
            send_sem=gs_sem.at[slot, j], recv_sem=gr_sem.at[slot, j],
            device_id=(other, me, rad), device_id_type=MESH)

    def halo_copies(slot):
        plan = (
            (csend.at[slot], crecv.at[slot, 0], (row, right, rad)),
            (csend.at[slot], crecv.at[slot, 1], (row, left, rad)),
            (rsend.at[slot, 0], rrecv.at[slot, 0], (row, me, above)),
            (rsend.at[slot, 1], rrecv.at[slot, 1], (row, me, below)),
        )
        return [
            pltpu.make_async_remote_copy(
                src_ref=src, dst_ref=dst, send_sem=hs_sem.at[slot, i],
                recv_sem=hr_sem.at[slot, i], device_id=peer, device_id_type=MESH)
            for i, (src, dst, peer) in enumerate(plan)
        ]

    order = sorted(range(nc), key=lambda d: -min(d, nc - d))

    def start_gather(slot):
        for d in order:
            gather_copy(slot, d).start()

    def pack(slot, k, q, packed):
        for c in range(5):
            rsend[slot, 0, c, k : k + 1, :] = q[c][rows - 1 : rows, :]
            rsend[slot, 1, c, k : k + 1, :] = q[c][0:1, :]
            place = c * ca + k
            packed = jnp.where(pair == place, pltpu.roll(q[c], 2 * place + 1, 1), packed)
        return packed

    zero = jnp.zeros((rows, cols), jnp.float32)
    packed = zero
    for c in range(5):
        far[c] = jnp.where(is_rotor, inflow_ref[c], outflow_ref[c])
    for k in range(ca):
        q = [flow_ref[0, c, axial(k)] for c in range(5)]
        for c in range(5):
            state[0, c, k] = q[c]
            if k == 0:
                gsend[0, c] = q[c]
        packed = pack(0, k, q, packed)
    csend[0] = packed
    pl.semaphore_wait(barrier, nc + 4)
    start_gather(0)
    for copy in halo_copies(0):
        copy.start()

    def stage(s, carry):
        step = lax.div(s, STAGES)
        phase = s - step * STAGES
        base = step * STAGES
        keep = jnp.where(phase == 0, 0.0, jnp.where(phase == 1, 0.75, 1.0 / 3.0)).astype(jnp.float32)
        mix = jnp.where(phase == 0, 1.0, jnp.where(phase == 1, 0.25, 2.0 / 3.0)).astype(jnp.float32)

        for copy in halo_copies(s):
            copy.wait_recv()
        merged = jnp.where(
            even, pltpu.roll(crecv[s, 1], cols - 1, 1), pltpu.roll(crecv[s, 0], 1, 1))

        def load(k):
            q = [state[s, c, k] for c in range(5)]
            prim = primitives(q)
            f, speed = normal_flux(q, prim, 0)
            return q, prim, f, speed

        def in_plane(k, q, prim):
            _, _, sound = prim
            speed = jnp.abs(prim[0][1]) + sound
            up, down = [], []
            for c in range(5):
                mirror = -q[c] if c == 2 else q[c]
                u = jnp.where(last_sub, rrecv[s, 1, c, k : k + 1, :], pltpu.roll(q[c], rows - 1, 0))
                d = jnp.where(first_sub, rrecv[s, 0, c, k : k + 1, :], pltpu.roll(q[c], 1, 0))
                up.append(jnp.where(wall_hi, mirror, u))
                down.append(jnp.where(wall_lo, mirror, d))
            fu, su = normal_flux(up, primitives(up), 1)
            fd, sd = normal_flux(down, primitives(down), 1)
            ju, jd = jump(speed, su, q, up), jump(sd, speed, down, q)
            acc = [(fu[c] - fd[c]) - (ju[c] - jd[c]) for c in range(5)]
            speed = jnp.abs(prim[0][2]) + sound
            after, before = [], []
            for c in range(5):
                place = c * ca + k
                edge = pltpu.roll(merged, cols - 1 - 2 * place, 1)
                after.append(jnp.where(last_lane, edge, pltpu.roll(q[c], cols - 1, 1)))
                before.append(jnp.where(first_lane, edge, pltpu.roll(q[c], 1, 1)))
            fa, sa = normal_flux(after, primitives(after), 2)
            fb, sb = normal_flux(before, primitives(before), 2)
            ja, jb = jump(speed, sa, q, after), jump(sb, speed, before, q)
            return [acc[c] + ((fa[c] - fb[c]) - (ja[c] - jb[c])) for c in range(5)]

        def finish(k, q, acc):
            new = []
            for c in range(5):
                advanced = q[c] + (-0.5 * COURANT) * acc[c]
                new.append(keep * state[base, c, k] + mix * advanced)
                state[s + 1, c, k] = new[c]
            return new

        q0, prim0, f0, s0 = load(0)
        here = load(1)
        j0 = jump(s0, here[3], q0, here[0])
        acc0 = in_plane(0, q0, prim0)
        acc0 = [acc0[c] + sigma * here[2][c] - j0[c] for c in range(5)]
        packed = zero
        toward_f, toward_j = f0, j0
        for k in range(1, ca):
            q, prim, f, speed = here
            if k + 1 < ca:
                here = load(k + 1)
            else:
                qf = [far[c] for c in range(5)]
                pf = primitives(qf)
                here = (qf, pf) + normal_flux(qf, pf, 0)
            j = jump(speed, here[3], q, here[0])
            acc = in_plane(k, q, prim)
            acc = [
                acc[c] + sigma * (here[2][c] - toward_f[c]) - (j[c] - toward_j[c]) for c in range(5)
            ]
            packed = pack(s + 1, k, finish(k, q, acc), packed)
            toward_f, toward_j = f, j

        offset = offsets_ref[step]
        cycle = nc * cols
        shift = jnp.where(is_rotor, offset, cycle - offset)
        start = lax.rem(me * cols + shift, cycle)
        block = lax.div(start, cols)
        turn = start - block * cols
        back = lax.rem(cols - turn, cols)
        following = lax.rem(block + 1, nc)
        for j in range(nc):
            gather_arrival(s, j).wait_recv()
        ghost = []
        want = jnp.where(lane >= turn, block, following)
        for c in range(5):
            both = grecv[s, 0, c]
            for j in range(1, nc):
                both = jnp.where(want == j, grecv[s, j, c], both)
            ghost.append(pltpu.roll(both, back, 1))
        swirl = ghost[3]
        ghost[4] = ghost[4] + sigma * swirl * blade + 0.5 * ghost[0] * blade * blade
        ghost[3] = swirl + sigma * ghost[0] * blade
        fg, sg = normal_flux(ghost, primitives(ghost), 0)
        jg = jump(sg, s0, ghost, q0)
        acc0 = [acc0[c] - sigma * fg[c] + jg[c] for c in range(5)]
        new = finish(0, q0, acc0)
        for c in range(5):
            gsend[s + 1, c] = new[c]

        @pl.when(s < total - 1)
        def _():
            start_gather(s + 1)

        csend[s + 1] = pack(s + 1, 0, new, packed)

        @pl.when(s < total - 1)
        def _():
            for copy in halo_copies(s + 1):
                copy.start()

        return carry

    lax.fori_loop(0, total, stage, 0)
    for k in range(ca):
        for c in range(5):
            out_ref[0, c, axial(k)] = state[total, c, k]

    def drain(s, carry):
        for d in range(nc):
            gather_copy(s, d).wait_send()
        for copy in halo_copies(s):
            copy.wait_send()
        return carry

    lax.fori_loop(0, total, drain, 0)


def solution(mesh):
    placed = (
        P("row", None, None, "rad", "circ"),
        P(None, "rad", "circ"),
        P(None, "rad", "circ"),
        P("rad"),
        P(),
    )
    nc, nr = mesh.shape["circ"], mesh.shape["rad"]

    def per_device(flow, inflow, outflow, wheel, offsets):
        _, comps, ca, rows, cols = flow.shape
        steps = offsets.shape[0]
        total = steps * STAGES
        vmem = pl.BlockSpec(memory_space=pltpu.VMEM)
        smem = pl.BlockSpec(memory_space=pltpu.SMEM)
        f32 = jnp.float32
        return pl.pallas_call(
            functools.partial(kernel, nc, nr, steps),
            out_shape=jax.ShapeDtypeStruct(flow.shape, f32),
            in_specs=[vmem, vmem, vmem, smem, smem],
            out_specs=vmem,
            scratch_shapes=[
                pltpu.VMEM((total + 1, comps, ca, rows, cols), f32),
                pltpu.VMEM((comps, rows, cols), f32),
                pltpu.VMEM((total + 1, comps, rows, cols), f32),
                pltpu.VMEM((total, nc, comps, rows, cols), f32),
                pltpu.VMEM((total + 1, rows, cols), f32),
                pltpu.VMEM((total, 2, rows, cols), f32),
                pltpu.VMEM((total + 1, 2, comps, ca, cols), f32),
                pltpu.VMEM((total, 2, comps, ca, cols), f32),
                pltpu.SemaphoreType.DMA((total, nc)),
                pltpu.SemaphoreType.DMA((total, nc)),
                pltpu.SemaphoreType.DMA((total, 4)),
                pltpu.SemaphoreType.DMA((total, 4)),
            ],
            compiler_params=pltpu.CompilerParams(
                collective_id=0, has_side_effects=True, vmem_limit_bytes=24 * 1024 * 1024),
        )(flow, inflow, outflow, wheel, offsets)

    return jax.shard_map(
        per_device,
        mesh=mesh,
        in_specs=placed,
        out_specs=P("row", None, None, "rad", "circ"),
        check_vma=False,
    )
```

time: 165 us -> 40.7 us (0.25)
  blocking collectives: 79.3 us -> 0 us
  starting transfers between devices: 63.5 us -> 0 us
  Pallas kernels: 0 us -> 36.1 us
  other arithmetic: 11.7 us -> 0 us
  loops' own time: 3.82 us -> 0 us
  waiting for transfers between devices: 2.13 us -> 0 us
    all_gather x6 -> x0, blocking collectives: 79.3 us -> none  [rotate_layer(): gathered = lax.all_gather(partner, 'circ', axis=2, tiled=True)]
    ppermute x30 -> x0, starting transfers between devices: 63.5 us -> none  [the longest x12 31.8 us: with_halo(): after = lax.ppermute(first, axis, down)]
    pallas_call x0 -> x1, Pallas kernels: none -> 36.1 us  [per_device(): pl.pallas_call(functools.partial(kernel, nc, nr, steps), out_shape=jax.Sh...]
    mul x104 -> x0, other arithmetic: 5.44 us -> none  [the longest x52 2.05 us: physical_flux(): velocity = field[1:4] * inverse]
    another operation x1 -> x0, loops' own time: 3.82 us -> none  [per_device(): field = lax.fori_loop(0, offsets.shape[0], one_step, field)]
    sub x18 -> x0, other arithmetic: 3.78 us -> none  [face_flux(): 0.5 * (flux_left + flux_right)]
    unnamed x22 -> x11, local copies, waits for them, and re-layouts: 1.54 us -> 4.35 us
    ppermute x30 -> x0, waiting for transfers between devices: 2.13 us -> none  [the longest x12 1.6 us: with_halo(): before = lax.ppermute(last, axis, up)]
  transfers between devices with their start and end apart: 30 -> 0, of which waited for: 7 -> 0; matrix products, arithmetic and copies ran while one was open for 4% -> 0% of each run, Pallas kernels for 0% -> 0%
where the time goes in v1:
time: 40.7 us; the launch traced here: 40.5 us
  Pallas kernels  36.1 us (89%)
  local copies, waits for them, and re-layouts  4.35 us (11%)
    pallas_call x1, Pallas kernels, per_device(): pl.pallas_call(functools.partial(kernel, nc, nr, steps), out_shape=jax.Sh...  36.1 us
    unnamed x11, local copies, waits for them, and re-layouts  4.35 us

profile of v1, /device:TPU:0, one launch (start us, length us, event | category | flops | bytes accessed | tf_op | source)
XLA Modules:
  0.0 40.5 jit_solution(16713933159825038070)
XLA Ops:
  0.0 0.0 copy-start
  0.0 0.9 %copy-done = f32[1,5,8,8,128]{4,3,2,1,0:T(8,128)S(1)} copy-done((f32[1,5,8,8,128]{4,3,2,1,0:T(8,128)S(1)}, f32[1,5,8,8,128]{4,3,2,1,0:T(8,128)}, u32[]{:S(2)}) %copy-start) | copy-done | bytes 163864
  0.9 0.0 copy-start.1
  0.9 0.7 %copy-done.1 = f32[5,8,128]{2,1,0:T(8,128)S(1)} copy-done((f32[5,8,128]{2,1,0:T(8,128)S(1)}, f32[5,8,128]{2,1,0:T(8,128)}, u32[]{:S(2)}) %copy-start.1) | copy-done | bytes 20504
  1.6 0.0 copy-start.2
  1.6 0.7 %copy-done.2 = f32[5,8,128]{2,1,0:T(8,128)S(1)} copy-done((f32[5,8,128]{2,1,0:T(8,128)S(1)}, f32[5,8,128]{2,1,0:T(8,128)}, u32[]{:S(2)}) %copy-start.2) | copy-done | bytes 20504
  2.4 0.0 copy-start.3
  2.4 0.7 %copy-done.3 = f32[8]{0:T(128)S(1)} copy-done((f32[8]{0:T(128)S(1)}, f32[8]{0:T(128)}, u32[]{:S(2)}) %copy-start.3) | copy-done | bytes 56
  3.0 0.0 copy-start.4
  3.0 0.7 %copy-done.4 = s32[2]{0:T(128)S(1)} copy-done((s32[2]{0:T(128)S(1)}, s32[2]{0:T(128)}, u32[]{:S(2)}) %copy-start.4) | copy-done | bytes 32
  3.7 36.1 %shard_map.55 = f32[1,5,8,8,128]{4,3,2,1,0:T(8,128)S(1)} custom-call(f32[1,5,8,8,128]{4,3,2,1,0:T(8,128)S(1)} %copy-done, f32[5,8,128]{2,1,0:T(8,128)S(1)} %copy-done.1, f32[5,8,128]{2,1,0:T(8,128)S(1)} %copy-done.2, f32[8]{0:T(128)S(1)} %copy-done.3, s32[2]{0:T(128)S(1)} %copy-done.4), custom_call_target="tpu_custom_call" | custom-call | tf_op jit(solution)/shard_map/pallas_call | solution.py:282
  39.8 0.7 %copy.7 = f32[1,5,8,8,128]{4,3,2,1,0:T(8,128)} copy(f32[1,5,8,8,128]{4,3,2,1,0:T(8,128)S(1)} %shard_map.55) | data formatting | bytes 327680
Async XLA Ops:
  0.0 0.9 %copy-start = (f32[1,5,8,8,128]{4,3,2,1,0:T(8,128)S(1)}, f32[1,5,8,8,128]{4,3,2,1,0:T(8,128)}, u32[]{:S(2)}) copy-start(f32[1,5,8,8,128]{4,3,2,1,0:T(8,128)} %flow_ref.1) | copy-start | bytes 491524
  0.9 0.7 %copy-start.1 = (f32[5,8,128]{2,1,0:T(8,128)S(1)}, f32[5,8,128]{2,1,0:T(8,128)}, u32[]{:S(2)}) copy-start(f32[5,8,128]{2,1,0:T(8,128)} %inflow_ref.1) | copy-start | bytes 61444
  1.6 0.7 %copy-start.2 = (f32[5,8,128]{2,1,0:T(8,128)S(1)}, f32[5,8,128]{2,1,0:T(8,128)}, u32[]{:S(2)}) copy-start(f32[5,8,128]{2,1,0:T(8,128)} %outflow_ref.1) | copy-start | bytes 61444
  2.4 0.7 %copy-start.3 = (f32[8]{0:T(128)S(1)}, f32[8]{0:T(128)}, u32[]{:S(2)}) copy-start(f32[8]{0:T(128)} %wheel_ref.1) | copy-start | bytes 100
  3.0 0.7 %copy-start.4 = (s32[2]{0:T(128)S(1)}, s32[2]{0:T(128)}, u32[]{:S(2)}) copy-start(s32[2]{0:T(128)} %offsets_ref.1) | copy-start | bytes 28

commit v2 on v1

--- a/solution.py
+++ b/solution.py
@@ -11,6 +11,12 @@
 COURANT = 0.1
 MESH = pl.DeviceIdType.MESH
 STAGES = 3
+CUT = 4
+
+
+def layer_groups(ca):
+    cut = min(1 + CUT, ca)
+    return [g for g in ([0], list(range(1, cut)), list(range(cut, ca))) if g]
 
 
 def primitives(q):
@@ -37,17 +43,26 @@
 
 def kernel(
     nc, nr, steps,
-    flow_ref, inflow_ref, outflow_ref, wheel_ref, offsets_ref,
+    flow_hbm, inflow_hbm, outflow_hbm, wheel_ref, offsets_ref,
     out_ref,
-    state, far, gsend, grecv, csend, crecv, rsend, rrecv,
-    gs_sem, gr_sem, hs_sem, hr_sem,
+    flow_ref, ends, in_sem,
+    state, far, gsend, grecv, csend, crecv, gs_sem, gr_sem, hs_sem, hr_sem, *rims,
 ):
+    inputs = [
+        pltpu.make_async_copy(src, dst, in_sem.at[i])
+        for i, (src, dst) in enumerate(
+            ((flow_hbm, flow_ref), (inflow_hbm, ends.at[0]), (outflow_hbm, ends.at[1])))
+    ]
+    for copy in inputs:
+        copy.start()
     ca, rows, cols = state.shape[2:]
     total = steps * STAGES
     row = lax.axis_index("row")
     me = lax.axis_index("circ")
     rad = lax.axis_index("rad")
     is_rotor = row == 0
+    groups = layer_groups(ca)
+    rsends, rrecvs = rims[: len(groups)], rims[len(groups) :]
     other = 1 - row
     right, left = lax.rem(me + 1, nc), lax.rem(me + nc - 1, nc)
     above, below = lax.rem(rad + 1, nr), lax.rem(rad + nr - 1, nr)
@@ -75,11 +90,14 @@
     def axial(k):
         return jnp.where(is_rotor, ca - 1 - k, k)
 
+    def target(d):
+        return jnp.where(2 * me < nc, nc - 1 - d, d)
+
     def gather_copy(slot, d):
         return pltpu.make_async_remote_copy(
             src_ref=gsend.at[slot], dst_ref=grecv.at[slot, me],
             send_sem=gs_sem.at[slot, d], recv_sem=gr_sem.at[slot, me],
-            device_id=(other, lax.rem(me + d, nc), rad), device_id_type=MESH)
+            device_id=(other, target(d), rad), device_id_type=MESH)
 
     def gather_arrival(slot, j):
         return pltpu.make_async_remote_copy(
@@ -87,50 +105,59 @@
             send_sem=gs_sem.at[slot, j], recv_sem=gr_sem.at[slot, j],
             device_id=(other, me, rad), device_id_type=MESH)
 
-    def halo_copies(slot):
+    def halo_copies(slot, g):
         plan = (
-            (csend.at[slot], crecv.at[slot, 0], (row, right, rad)),
-            (csend.at[slot], crecv.at[slot, 1], (row, left, rad)),
-            (rsend.at[slot, 0], rrecv.at[slot, 0], (row, me, above)),
-            (rsend.at[slot, 1], rrecv.at[slot, 1], (row, me, below)),
+            (csend.at[slot, g], crecv.at[slot, g, 0], (row, right, rad)),
+            (csend.at[slot, g], crecv.at[slot, g, 1], (row, left, rad)),
+            (rsends[g].at[slot, 0], rrecvs[g].at[slot, 0], (row, me, above)),
+            (rsends[g].at[slot, 1], rrecvs[g].at[slot, 1], (row, me, below)),
         )
         return [
             pltpu.make_async_remote_copy(
-                src_ref=src, dst_ref=dst, send_sem=hs_sem.at[slot, i],
-                recv_sem=hr_sem.at[slot, i], device_id=peer, device_id_type=MESH)
+                src_ref=src, dst_ref=dst, send_sem=hs_sem.at[slot, g, i],
+                recv_sem=hr_sem.at[slot, g, i], device_id=peer, device_id_type=MESH)
             for i, (src, dst, peer) in enumerate(plan)
         ]
 
-    order = sorted(range(nc), key=lambda d: -min(d, nc - d))
+    def start_halos(slot, g):
+        for copy in halo_copies(slot, g):
+            copy.start()
 
     def start_gather(slot):
-        for d in order:
+        for d in range(nc):
             gather_copy(slot, d).start()
+
+    def position(k, c):
+        g = next(i for i, group in enumerate(groups) if k in group)
+        return g, c * len(groups[g]) + groups[g].index(k)
 
     def pack(slot, k, q, packed):
         for c in range(5):
-            rsend[slot, 0, c, k : k + 1, :] = q[c][rows - 1 : rows, :]
-            rsend[slot, 1, c, k : k + 1, :] = q[c][0:1, :]
-            place = c * ca + k
+            g, place = position(k, c)
+            rsends[g][slot, 0, place : place + 1, :] = q[c][rows - 1 : rows, :]
+            rsends[g][slot, 1, place : place + 1, :] = q[c][0:1, :]
             packed = jnp.where(pair == place, pltpu.roll(q[c], 2 * place + 1, 1), packed)
         return packed
 
     zero = jnp.zeros((rows, cols), jnp.float32)
-    packed = zero
+    for copy in inputs:
+        copy.wait()
     for c in range(5):
-        far[c] = jnp.where(is_rotor, inflow_ref[c], outflow_ref[c])
-    for k in range(ca):
-        q = [flow_ref[0, c, axial(k)] for c in range(5)]
-        for c in range(5):
-            state[0, c, k] = q[c]
-            if k == 0:
-                gsend[0, c] = q[c]
-        packed = pack(0, k, q, packed)
-    csend[0] = packed
+        far[c] = jnp.where(is_rotor, ends[0, c], ends[1, c])
+    for g, group in enumerate(groups):
+        packed = zero
+        for k in group:
+            q = [flow_ref[0, c, axial(k)] for c in range(5)]
+            for c in range(5):
+                state[0, c, k] = q[c]
+                if k == 0:
+                    gsend[0, c] = q[c]
+            packed = pack(0, k, q, packed)
+        csend[0, g] = packed
     pl.semaphore_wait(barrier, nc + 4)
     start_gather(0)
-    for copy in halo_copies(0):
-        copy.start()
+    for g in list(range(1, len(groups))) + [0]:
+        start_halos(0, g)
 
     def stage(s, carry):
         step = lax.div(s, STAGES)
@@ -139,10 +166,18 @@
         keep = jnp.where(phase == 0, 0.0, jnp.where(phase == 1, 0.75, 1.0 / 3.0)).astype(jnp.float32)
         mix = jnp.where(phase == 0, 1.0, jnp.where(phase == 1, 0.25, 2.0 / 3.0)).astype(jnp.float32)
 
-        for copy in halo_copies(s):
-            copy.wait_recv()
-        merged = jnp.where(
-            even, pltpu.roll(crecv[s, 1], cols - 1, 1), pltpu.roll(crecv[s, 0], 1, 1))
+        def halos(g):
+            for copy in halo_copies(s, g):
+                copy.wait_recv()
+            return jnp.where(
+                even, pltpu.roll(crecv[s, g, 1], cols - 1, 1), pltpu.roll(crecv[s, g, 0], 1, 1))
+
+        def send(g, packed):
+            csend[s + 1, g] = packed
+
+            @pl.when(s < total - 1)
+            def _():
+                start_halos(s + 1, g)
 
         def load(k):
             q = [state[s, c, k] for c in range(5)]
@@ -150,14 +185,16 @@
             f, speed = normal_flux(q, prim, 0)
             return q, prim, f, speed
 
-        def in_plane(k, q, prim):
+        def in_plane(k, q, prim, merged):
             _, _, sound = prim
             speed = jnp.abs(prim[0][1]) + sound
             up, down = [], []
             for c in range(5):
                 mirror = -q[c] if c == 2 else q[c]
-                u = jnp.where(last_sub, rrecv[s, 1, c, k : k + 1, :], pltpu.roll(q[c], rows - 1, 0))
-                d = jnp.where(first_sub, rrecv[s, 0, c, k : k + 1, :], pltpu.roll(q[c], 1, 0))
+                g, place = position(k, c)
+                rim = rrecvs[g]
+                u = jnp.where(last_sub, rim[s, 1, place : place + 1, :], pltpu.roll(q[c], rows - 1, 0))
+                d = jnp.where(first_sub, rim[s, 0, place : place + 1, :], pltpu.roll(q[c], 1, 0))
                 up.append(jnp.where(wall_hi, mirror, u))
                 down.append(jnp.where(wall_lo, mirror, d))
             fu, su = normal_flux(up, primitives(up), 1)
@@ -167,7 +204,7 @@
             speed = jnp.abs(prim[0][2]) + sound
             after, before = [], []
             for c in range(5):
-                place = c * ca + k
+                _, place = position(k, c)
                 edge = pltpu.roll(merged, cols - 1 - 2 * place, 1)
                 after.append(jnp.where(last_lane, edge, pltpu.roll(q[c], cols - 1, 1)))
                 before.append(jnp.where(first_lane, edge, pltpu.roll(q[c], 1, 1)))
@@ -187,25 +224,30 @@
         q0, prim0, f0, s0 = load(0)
         here = load(1)
         j0 = jump(s0, here[3], q0, here[0])
-        acc0 = in_plane(0, q0, prim0)
-        acc0 = [acc0[c] + sigma * here[2][c] - j0[c] for c in range(5)]
-        packed = zero
+        axial0 = [sigma * here[2][c] - j0[c] for c in range(5)]
         toward_f, toward_j = f0, j0
-        for k in range(1, ca):
-            q, prim, f, speed = here
-            if k + 1 < ca:
-                here = load(k + 1)
-            else:
-                qf = [far[c] for c in range(5)]
-                pf = primitives(qf)
-                here = (qf, pf) + normal_flux(qf, pf, 0)
-            j = jump(speed, here[3], q, here[0])
-            acc = in_plane(k, q, prim)
-            acc = [
-                acc[c] + sigma * (here[2][c] - toward_f[c]) - (j[c] - toward_j[c]) for c in range(5)
-            ]
-            packed = pack(s + 1, k, finish(k, q, acc), packed)
-            toward_f, toward_j = f, j
+        for g in range(1, len(groups)):
+            merged = halos(g)
+            packed = zero
+            for k in groups[g]:
+                q, prim, f, speed = here
+                if k + 1 < ca:
+                    here = load(k + 1)
+                else:
+                    qf = [far[c] for c in range(5)]
+                    pf = primitives(qf)
+                    here = (qf, pf) + normal_flux(qf, pf, 0)
+                j = jump(speed, here[3], q, here[0])
+                acc = in_plane(k, q, prim, merged)
+                acc = [
+                    acc[c] + sigma * (here[2][c] - toward_f[c]) - (j[c] - toward_j[c])
+                    for c in range(5)
+                ]
+                packed = pack(s + 1, k, finish(k, q, acc), packed)
+                toward_f, toward_j = f, j
+            send(g, packed)
+        acc0 = in_plane(0, q0, prim0, halos(0))
+        acc0 = [acc0[c] + axial0[c] for c in range(5)]
 
         offset = offsets_ref[step]
         cycle = nc * cols
@@ -238,13 +280,7 @@
         def _():
             start_gather(s + 1)
 
-        csend[s + 1] = pack(s + 1, 0, new, packed)
-
-        @pl.when(s < total - 1)
-        def _():
-            for copy in halo_copies(s + 1):
-                copy.start()
-
+        send(0, pack(s + 1, 0, new, zero))
         return carry
 
     lax.fori_loop(0, total, stage, 0)
@@ -255,8 +291,9 @@
     def drain(s, carry):
         for d in range(nc):
             gather_copy(s, d).wait_send()
-        for copy in halo_copies(s):
-            copy.wait_send()
+        for g in range(len(groups)):
+            for copy in halo_copies(s, g):
+                copy.wait_send()
         return carry
 
     lax.fori_loop(0, total, drain, 0)
@@ -278,25 +315,31 @@
         total = steps * STAGES
         vmem = pl.BlockSpec(memory_space=pltpu.VMEM)
         smem = pl.BlockSpec(memory_space=pltpu.SMEM)
+        hbm = pl.BlockSpec(memory_space=pltpu.HBM)
         f32 = jnp.float32
+        groups = layer_groups(ca)
+        rims = [-(-comps * len(group) // 8) * 8 for group in groups]
         return pl.pallas_call(
             functools.partial(kernel, nc, nr, steps),
             out_shape=jax.ShapeDtypeStruct(flow.shape, f32),
-            in_specs=[vmem, vmem, vmem, smem, smem],
+            in_specs=[hbm, hbm, hbm, smem, smem],
             out_specs=vmem,
             scratch_shapes=[
+                pltpu.VMEM(flow.shape, f32),
+                pltpu.VMEM((2, comps, rows, cols), f32),
+                pltpu.SemaphoreType.DMA((3,)),
                 pltpu.VMEM((total + 1, comps, ca, rows, cols), f32),
                 pltpu.VMEM((comps, rows, cols), f32),
                 pltpu.VMEM((total + 1, comps, rows, cols), f32),
                 pltpu.VMEM((total, nc, comps, rows, cols), f32),
-                pltpu.VMEM((total + 1, rows, cols), f32),
-                pltpu.VMEM((total, 2, rows, cols), f32),
-                pltpu.VMEM((total + 1, 2, comps, ca, cols), f32),
-                pltpu.VMEM((total, 2, comps, ca, cols), f32),
+                pltpu.VMEM((total + 1, len(groups), rows, cols), f32),
+                pltpu.VMEM((total, len(groups), 2, rows, cols), f32),
                 pltpu.SemaphoreType.DMA((total, nc)),
                 pltpu.SemaphoreType.DMA((total, nc)),
-                pltpu.SemaphoreType.DMA((total, 4)),
-                pltpu.SemaphoreType.DMA((total, 4)),
+                pltpu.SemaphoreType.DMA((total, len(groups), 4)),
+                pltpu.SemaphoreType.DMA((total, len(groups), 4)),
+                *[pltpu.VMEM((total + 1, 2, rim, cols), f32) for rim in rims],
+                *[pltpu.VMEM((total, 2, rim, cols), f32) for rim in rims],
             ],
             compiler_params=pltpu.CompilerParams(
                 collective_id=0, has_side_effects=True, vmem_limit_bytes=24 * 1024 * 1024),

time: 40.7 us -> 40.6 us (level)
  no operation moved by 1% of the time
where the time goes in v2:
time: 40.6 us; the launch traced here: 40.3 us
  Pallas kernels  36 us (89%)
  local copies, waits for them, and re-layouts  4.35 us (11%)
    pallas_call x1, Pallas kernels, per_device(): pl.pallas_call(functools.partial(kernel, nc, nr, steps), out_shape=jax.Sh...  36 us
    unnamed x11, local copies, waits for them, and re-layouts  4.35 us

profile of v2, /device:TPU:0, one launch (start us, length us, event | category | flops | bytes accessed | tf_op | source)
XLA Modules:
  0.0 40.3 jit_solution(1618485960978684489)
XLA Ops:
  0.0 0.0 copy-start
  0.0 0.9 %copy-done = f32[1,5,8,8,128]{4,3,2,1,0:T(8,128)S(1)} copy-done((f32[1,5,8,8,128]{4,3,2,1,0:T(8,128)S(1)}, f32[1,5,8,8,128]{4,3,2,1,0:T(8,128)}, u32[]{:S(2)}) %copy-start) | copy-done | bytes 163864
  0.9 0.0 copy-start.1
  0.9 0.7 %copy-done.1 = f32[5,8,128]{2,1,0:T(8,128)S(1)} copy-done((f32[5,8,128]{2,1,0:T(8,128)S(1)}, f32[5,8,128]{2,1,0:T(8,128)}, u32[]{:S(2)}) %copy-start.1) | copy-done | bytes 20504
  1.6 0.0 copy-start.2
  1.6 0.7 %copy-done.2 = f32[5,8,128]{2,1,0:T(8,128)S(1)} copy-done((f32[5,8,128]{2,1,0:T(8,128)S(1)}, f32[5,8,128]{2,1,0:T(8,128)}, u32[]{:S(2)}) %copy-start.2) | copy-done | bytes 20504
  2.4 0.0 copy-start.3
  2.4 0.7 %copy-done.3 = f32[8]{0:T(128)S(1)} copy-done((f32[8]{0:T(128)S(1)}, f32[8]{0:T(128)}, u32[]{:S(2)}) %copy-start.3) | copy-done | bytes 56
  3.0 0.0 copy-start.4
  3.0 0.7 %copy-done.4 = s32[2]{0:T(128)S(1)} copy-done((s32[2]{0:T(128)S(1)}, s32[2]{0:T(128)}, u32[]{:S(2)}) %copy-start.4) | copy-done | bytes 32
  3.7 36.0 %shard_map.55 = f32[1,5,8,8,128]{4,3,2,1,0:T(8,128)S(1)} custom-call(f32[1,5,8,8,128]{4,3,2,1,0:T(8,128)S(1)} %copy-done, f32[5,8,128]{2,1,0:T(8,128)S(1)} %copy-done.1, f32[5,8,128]{2,1,0:T(8,128)S(1)} %copy-done.2, f32[8]{0:T(128)S(1)} %copy-done.3, s32[2]{0:T(128)S(1)} %copy-done.4), custom_call_target="tpu_custom_call" | custom-call | tf_op jit(solution)/shard_map/pallas_call | solution.py:322
  39.7 0.7 %copy.7 = f32[1,5,8,8,128]{4,3,2,1,0:T(8,128)} copy(f32[1,5,8,8,128]{4,3,2,1,0:T(8,128)S(1)} %shard_map.55) | data formatting | bytes 327680
Async XLA Ops:
  0.0 0.9 %copy-start = (f32[1,5,8,8,128]{4,3,2,1,0:T(8,128)S(1)}, f32[1,5,8,8,128]{4,3,2,1,0:T(8,128)}, u32[]{:S(2)}) copy-start(f32[1,5,8,8,128]{4,3,2,1,0:T(8,128)} %flow_hbm.1) | copy-start | bytes 491524
  0.9 0.7 %copy-start.1 = (f32[5,8,128]{2,1,0:T(8,128)S(1)}, f32[5,8,128]{2,1,0:T(8,128)}, u32[]{:S(2)}) copy-start(f32[5,8,128]{2,1,0:T(8,128)} %inflow_hbm.1) | copy-start | bytes 61444
  1.6 0.7 %copy-start.2 = (f32[5,8,128]{2,1,0:T(8,128)S(1)}, f32[5,8,128]{2,1,0:T(8,128)}, u32[]{:S(2)}) copy-start(f32[5,8,128]{2,1,0:T(8,128)} %outflow_hbm.1) | copy-start | bytes 61444
  2.4 0.7 %copy-start.3 = (f32[8]{0:T(128)S(1)}, f32[8]{0:T(128)}, u32[]{:S(2)}) copy-start(f32[8]{0:T(128)} %wheel_ref.1) | copy-start | bytes 100
  3.0 0.7 %copy-start.4 = (s32[2]{0:T(128)S(1)}, s32[2]{0:T(128)}, u32[]{:S(2)}) copy-start(s32[2]{0:T(128)} %offsets_ref.1) | copy-start | bytes 28

commit v3 on v2

--- a/solution.py
+++ b/solution.py
@@ -11,7 +11,7 @@
 COURANT = 0.1
 MESH = pl.DeviceIdType.MESH
 STAGES = 3
-CUT = 4
+CUT = 7
 
 
 def layer_groups(ca):
@@ -276,11 +276,17 @@
         for c in range(5):
             gsend[s + 1, c] = new[c]
 
+        csend[s + 1, 0] = pack(s + 1, 0, new, zero)
+
         @pl.when(s < total - 1)
         def _():
+            copies = halo_copies(s + 1, 0)
+            for copy in copies[:2]:
+                copy.start()
             start_gather(s + 1)
-
-        send(0, pack(s + 1, 0, new, zero))
+            for copy in copies[2:]:
+                copy.start()
+
         return carry
 
     lax.fori_loop(0, total, stage, 0)
@@ -342,7 +348,7 @@
                 *[pltpu.VMEM((total, 2, rim, cols), f32) for rim in rims],
             ],
             compiler_params=pltpu.CompilerParams(
-                collective_id=0, has_side_effects=True, vmem_limit_bytes=24 * 1024 * 1024),
+                collective_id=0, has_side_effects=True, vmem_limit_bytes=60 * 1024 * 1024),
         )(flow, inflow, outflow, wheel, offsets)
 
     return jax.shard_map(

time: 40.6 us -> 35.8 us (0.88)
  local copies, waits for them, and re-layouts: 4.35 us -> 1.59 us
  Pallas kernels: 36 us -> 34 us
    unnamed x11 -> x1, local copies, waits for them, and re-layouts: 4.35 us -> 1.59 us
    pallas_call x1, Pallas kernels: 36 us -> 34 us  [per_device(): pl.pallas_call(functools.partial(kernel, nc, nr, steps), out_shape=jax.Sh...]
where the time goes in v3:
time: 35.8 us; the launch traced here: 35.6 us
  Pallas kernels  34 us (95%)
  local copies, waits for them, and re-layouts  1.59 us (4%)
    pallas_call x1, Pallas kernels, per_device(): pl.pallas_call(functools.partial(kernel, nc, nr, steps), out_shape=jax.Sh...  34 us
    unnamed x1, local copies, waits for them, and re-layouts  1.59 us

profile of v3, /device:TPU:0, one launch (start us, length us, event | category | flops | bytes accessed | tf_op | source)
XLA Modules:
  0.0 35.6 jit_solution(9291706479103521954)
XLA Ops:
  0.0 34.0 %shard_map.55 = f32[1,5,8,8,128]{4,3,2,1,0:T(8,128)} custom-call(f32[1,5,8,8,128]{4,3,2,1,0:T(8,128)} %flow_hbm.1, f32[5,8,128]{2,1,0:T(8,128)} %inflow_hbm.1, f32[5,8,128]{2,1,0:T(8,128)} %outflow_hbm.1, f32[8]{0:T(128)} %wheel_ref.1, s32[2]{0:T(128)} %offsets_ref.1), custom_call_target="tpu_custom_call" | custom-call | tf_op jit(solution)/shard_map/pallas_call | solution.py:328
  34.0 1.6 %copy.7 = f32[1,5,8,8,128]{4,3,2,1,0:T(8,128)} copy(f32[1,5,8,8,128]{4,3,2,1,0:T(8,128)} %shard_map.55) | data formatting | bytes 327680

commit v4 on v3

--- a/solution.py
+++ b/solution.py
@@ -11,7 +11,7 @@
 COURANT = 0.1
 MESH = pl.DeviceIdType.MESH
 STAGES = 3
-CUT = 7
+CUT = 4
 
 
 def layer_groups(ca):
@@ -281,11 +281,9 @@
         @pl.when(s < total - 1)
         def _():
             copies = halo_copies(s + 1, 0)
-            for copy in copies[:2]:
+            for copy in copies:
                 copy.start()
             start_gather(s + 1)
-            for copy in copies[2:]:
-                copy.start()
 
         return carry
 

time: 35.8 us -> 35.7 us (level)
  no operation moved by 1% of the time
where the time goes in v4:
time: 35.7 us; the launch traced here: 35.6 us
  Pallas kernels  34 us (95%)
  local copies, waits for them, and re-layouts  1.59 us (4%)
    pallas_call x1, Pallas kernels, per_device(): pl.pallas_call(functools.partial(kernel, nc, nr, steps), out_shape=jax.Sh...  34 us
    unnamed x1, local copies, waits for them, and re-layouts  1.59 us

profile of v4, /device:TPU:0, one launch (start us, length us, event | category | flops | bytes accessed | tf_op | source)
XLA Modules:
  0.0 35.6 jit_solution(3631235727684064195)
XLA Ops:
  0.0 34.0 %shard_map.55 = f32[1,5,8,8,128]{4,3,2,1,0:T(8,128)} custom-call(f32[1,5,8,8,128]{4,3,2,1,0:T(8,128)} %flow_hbm.1, f32[5,8,128]{2,1,0:T(8,128)} %inflow_hbm.1, f32[5,8,128]{2,1,0:T(8,128)} %outflow_hbm.1, f32[8]{0:T(128)} %wheel_ref.1, s32[2]{0:T(128)} %offsets_ref.1), custom_call_target="tpu_custom_call" | custom-call | tf_op jit(solution)/shard_map/pallas_call | solution.py:326
  34.0 1.6 %copy.7 = f32[1,5,8,8,128]{4,3,2,1,0:T(8,128)} copy(f32[1,5,8,8,128]{4,3,2,1,0:T(8,128)} %shard_map.55) | data formatting | bytes 327680

commit v5 on v4

--- a/solution.py
+++ b/solution.py
@@ -11,7 +11,7 @@
 COURANT = 0.1
 MESH = pl.DeviceIdType.MESH
 STAGES = 3
-CUT = 4
+CUT = 7
 
 
 def layer_groups(ca):
@@ -91,7 +91,7 @@
         return jnp.where(is_rotor, ca - 1 - k, k)
 
     def target(d):
-        return jnp.where(2 * me < nc, nc - 1 - d, d)
+        return lax.rem(me + d, nc)
 
     def gather_copy(slot, d):
         return pltpu.make_async_remote_copy(

time: 35.7 us -> 35.8 us (level)
  no operation moved by 1% of the time
where the time goes in v5:
time: 35.8 us; the launch traced here: 35.6 us
  Pallas kernels  34 us (95%)
  local copies, waits for them, and re-layouts  1.59 us (4%)
    pallas_call x1, Pallas kernels, per_device(): pl.pallas_call(functools.partial(kernel, nc, nr, steps), out_shape=jax.Sh...  34 us
    unnamed x1, local copies, waits for them, and re-layouts  1.59 us

profile of v5, /device:TPU:0, one launch (start us, length us, event | category | flops | bytes accessed | tf_op | source)
XLA Modules:
  0.0 35.6 jit_solution(17462987679494047927)
XLA Ops:
  0.0 34.0 %shard_map.55 = f32[1,5,8,8,128]{4,3,2,1,0:T(8,128)} custom-call(f32[1,5,8,8,128]{4,3,2,1,0:T(8,128)} %flow_hbm.1, f32[5,8,128]{2,1,0:T(8,128)} %inflow_hbm.1, f32[5,8,128]{2,1,0:T(8,128)} %outflow_hbm.1, f32[8]{0:T(128)} %wheel_ref.1, s32[2]{0:T(128)} %offsets_ref.1), custom_call_target="tpu_custom_call" | custom-call | tf_op jit(solution)/shard_map/pallas_call | solution.py:326
  34.0 1.6 %copy.7 = f32[1,5,8,8,128]{4,3,2,1,0:T(8,128)} copy(f32[1,5,8,8,128]{4,3,2,1,0:T(8,128)} %shard_map.55) | data formatting | bytes 327680
